TPU v7x, 32 devices: a whole 2x2x4 slice. The times are simulated.
32 devices in a mesh: sub: 8 (over z, core), front: 4 (over y, x).
Axes of the slice: x: 2, y: 2, z: 4, core: 2. Of those that a mesh axis runs over, the one named last changes fastest.
Arguments:
- noise_root: float32 [16, 128, 256], P('front', 'sub'), may hold values from -6 to 6
- inverse_root: float32 [16, 256, 256], P('front'), may hold values from -0.125 to 1.6, as said below
- up_root: float32 [16, 256, 128], P('front'), may hold values from -0.1875 to 0.1875
- left_root: float32 [16, 256, 128], P('front'), may hold values from -0.5 to 0.5
- rank_root: int32 [4], P('front'), may hold values from 64 to 128
- basis_root: float32 [16, 256, 128], P('front'), may hold values from -0.1875 to 0.1875
- noise_child: float32 [256, 128, 256], P(('sub', 'front')), may hold values from -6 to 6
- inverse_child: float32 [256, 256, 256], P(('sub', 'front')), may hold values from -0.125 to 1.6, as said below
- up_child: float32 [256, 256, 128], P(('sub', 'front')), may hold values from -0.125 to 0.125
- left_child: float32 [256, 256, 128], P(('sub', 'front')), may hold values from -0.5 to 0.5
- rank_child: int32 [32], P(('sub', 'front')), may hold values from 64 to 128
- couple: float32 [32, 4, 8, 256, 128], P(('sub', 'front')), may hold values from -0.125 to 0.125
- pattern: int32 [32, 4], P(('sub', 'front')), may hold values from 0 to 3, as said below
- couple_rank: int32 [32, 4], P(('sub', 'front')), may hold values from 64 to 128
Outputs:
- solved_root: float32 [16, 128, 256], P('front', 'sub')
- solved_child: float32 [256, 128, 256], P(('sub', 'front'))
Inputs may be any that keep to these rules, and one draw needn't show every extreme that they name: `pattern`: each row names 4 different root panels, the first being the row's own panel index (row modulo 4). `inverse_root`: each tile is lower triangular with a positive diagonal. `inverse_child`: each tile is lower triangular with a positive diagonal.
All inputs are finite; a program needn't handle non-finite values.
Results may differ from a plain program's by a relative error of at most 0.00022.
Values sent between devices are 32-bit elements; how exact they have to be, the bound alone decides.
A program may use at most 64 MiB of HBM per device.

v0:
```python
import jax
import jax.numpy as jnp
from jax import lax
from jax.sharding import PartitionSpec as P

PRECISE = lax.Precision.HIGHEST


def shifted(value, axis, steps):
    count = lax.axis_size(axis)
    initial, last = (max(0, -steps), min(count, count - steps))
    return lax.ppermute(value, axis, [(source, source + steps) for source in range(initial, last)])


def keep_mask(rank_cut, width):
    levels = lax.broadcasted_iota(jnp.int32, rank_cut.shape + (width,), rank_cut.ndim)
    return (levels < rank_cut[..., None]).astype(jnp.float32)


def operator_terms(inverse, upward, leftward, keeper):
    carried = jnp.einsum("tbk,tbc->tkc", leftward, inverse, precision=PRECISE)
    mixing = -jnp.einsum("tkc,tcl->kl", carried, upward, precision=PRECISE) * keeper
    return (carried, mixing)


def source_terms(source, inverse, upward, keeper):
    solved = jnp.einsum("tsb,tbc->tsc", source, inverse, precision=PRECISE)
    opening = jnp.einsum("tsc,tck->sk", solved, upward, precision=PRECISE) * keeper
    return (solved, opening)


def carry_in(opening, mixing, at_root):
    front_count = lax.axis_size("front")

    def advance(turn, arrived):
        outgoing = opening + jnp.dot(arrived, mixing, precision=PRECISE)
        if at_root:
            return shifted(outgoing, "front", -1)
        return shifted(outgoing, "front", -1)

    incoming = lax.fori_loop(0, front_count - 1, advance, jnp.zeros_like(opening))
    return incoming


def body(
    noise_root,
    inverse_root,
    up_root,
    left_root,
    rank_root,
    basis_root,
    noise_child,
    inverse_child,
    up_child,
    left_child,
    rank_child,
    couple,
    pattern,
    couple_rank,
):
    width = up_root.shape[-1]
    root_keep = keep_mask(rank_root, width)[0]
    child_keep = keep_mask(rank_child, width)[0]
    root_carried, root_mixing = operator_terms(inverse_root, up_root, left_root, root_keep)
    child_carried, child_mixing = operator_terms(inverse_child, up_child, left_child, child_keep)
    root_solved, root_opening = source_terms(noise_root, inverse_root, up_root, root_keep)
    root_message = carry_in(root_opening, root_mixing, True)
    solved_root = root_solved - jnp.einsum(
        "sk,tkc->tsc", root_message, root_carried, precision=PRECISE
    )
    projected = jnp.einsum("tsc,tck->sk", solved_root, basis_root, precision=PRECISE)
    samples = lax.all_gather(projected, "sub", axis=0, tiled=True)
    all_projected = lax.all_gather(samples[None], "front", axis=0, tiled=True)
    chosen = all_projected[pattern[0]] * keep_mask(couple_rank[0], width)[:, None, :]
    update = jnp.einsum("msk,mtbk->tsb", chosen, couple[0], precision=PRECISE)
    child_solved, child_opening = source_terms(
        noise_child - update, inverse_child, up_child, child_keep
    )
    child_message = carry_in(child_opening, child_mixing, False)
    solved_child = child_solved - jnp.einsum(
        "sk,tkc->tsc", child_message, child_carried, precision=PRECISE
    )
    return (solved_root, solved_child)


def solution(mesh):
    placed = (
        P("front", "sub", None),
        P("front", None, None),
        P("front", None, None),
        P("front", None, None),
        P("front"),
        P("front", None, None),
        P(("sub", "front"), None, None),
        P(("sub", "front"), None, None),
        P(("sub", "front"), None, None),
        P(("sub", "front"), None, None),
        P(("sub", "front")),
        P(("sub", "front"), None, None, None, None),
        P(("sub", "front"), None),
        P(("sub", "front"), None),
    )
    return jax.shard_map(
        body,
        mesh=mesh,
        in_specs=placed,
        out_specs=(P("front", "sub", None), P(("sub", "front"), None, None)),
        check_vma=False,
    )
```

profile of v0, /device:TPU:0, one launch (start us, length us, event | category | flops | bytes accessed | tf_op | source)
XLA Modules:
  0.0 92.8 jit_solution(1600470163893611017)
XLA Ops:
  3.6 1.9 %fusion.23 = f32[4,16,256]{2,1,0:T(8,128)S(1)} fusion(f32[4,16,256]{2,1,0:T(8,128)} %param.18, f32[4,256,256]{2,1,0:T(8,128)} %param.19), kind=kOutput, calls=%fused_computation.34 | convolution fusion | flops 50331648 | bytes 1179648 | tf_op jit(solution)/shard_map/tsb,tbc->tsc/dot_general | solution.py:27
  5.5 1.4 %fusion.15 = f32[16,128]{1,0:T(8,128)S(1)} fusion(f32[4,16,256]{2,1,0:T(8,128)S(1)} %fusion.23, f32[4,256,128]{2,1,0:T(8,128)} %param.20, f32[128]{0:T(128)S(1)} %compare_convert_fusion.1), kind=kOutput, calls=%fused_computation.21 | convolution fusion | flops 25167872 | bytes 598528 | tf_op jit(solution)/shard_map/tsc,tck->sk/dot_general | solution.py:28
  6.9 2.1 %fusion.24 = f32[4,128,256]{2,1,0:T(8,128)S(1)} fusion(f32[4,256,128]{2,1,0:T(8,128)} %param.21, f32[4,256,256]{2,1,0:T(8,128)S(1)} %copy-done.3), kind=kOutput, calls=%fused_computation.35 | convolution fusion | flops 402653184 | bytes 2097152 | tf_op jit(solution)/shard_map/tbk,tbc->tkc/dot_general | solution.py:21
  9.7 19.9 %while.20 = (s32[]{:T(128)}, f32[16,128]{1,0:T(8,128)S(1)}, f32[128,128]{1,0:T(8,128)S(1)}, f32[16,128]{1,0:T(8,128)S(1)}, s32[]{:T(128)}) while((s32[]{:T(128)}, f32[16,128]{1,0:T(8,128)S(1)}, f32[128,128]{1,0:T(8,128)S(1)}, f32[16,128]{1,0:T(8,128)S(1)}, s32[]{:T(128)}) %tuple.35), condition=%wide.region_1.0_spmd, body=%wide.region_0.0_spmd.sunk | while | flops 3147778 | bytes 122981 | solution.py:41
  9.9 1.3 %collective-permute-start = (f32[16,128]{1,0:T(8,128)S(1)}, f32[16,128]{1,0:T(8,128)S(1)}, u32[]{:S(2)}, u32[]{:S(2)}) collective-permute-start(f32[16,128]{1,0:T(8,128)S(1)} %convolution_add_fusion.4), channel_id=1, source_target_pairs={{1,0},{2,1},{3,2},{5,4},{6,5},{7,6},{9,8},{10,9},{11,10},{13,12},{... | collective-permute-start | bytes 24584 | tf_op jit(solution)/shard_map/while/body/eval_jaxpr/ppermute | solution.py:12
  11.2 5.2 %collective-permute-done = f32[16,128]{1,0:T(8,128)S(1)} collective-permute-done((f32[16,128]{1,0:T(8,128)S(1)}, f32[16,128]{1,0:T(8,128)S(1)}, u32[]{:S(2)}, u32[]{:S(2)}) %collective-permute-start) | collective-permute-done | bytes 8224 | tf_op jit(solution)/shard_map/while/body/eval_jaxpr/ppermute | solution.py:12
  16.5 1.3 %collective-permute-start = (f32[16,128]{1,0:T(8,128)S(1)}, f32[16,128]{1,0:T(8,128)S(1)}, u32[]{:S(2)}, u32[]{:S(2)}) collective-permute-start(f32[16,128]{1,0:T(8,128)S(1)} %convolution_add_fusion.4), channel_id=1, source_target_pairs={{1,0},{2,1},{3,2},{5,4},{6,5},{7,6},{9,8},{10,9},{11,10},{13,12},{... | collective-permute-start | bytes 24584 | tf_op jit(solution)/shard_map/while/body/eval_jaxpr/ppermute | solution.py:12
  17.8 5.1 %collective-permute-done = f32[16,128]{1,0:T(8,128)S(1)} collective-permute-done((f32[16,128]{1,0:T(8,128)S(1)}, f32[16,128]{1,0:T(8,128)S(1)}, u32[]{:S(2)}, u32[]{:S(2)}) %collective-permute-start) | collective-permute-done | bytes 8224 | tf_op jit(solution)/shard_map/while/body/eval_jaxpr/ppermute | solution.py:12
  23.1 1.3 %collective-permute-start = (f32[16,128]{1,0:T(8,128)S(1)}, f32[16,128]{1,0:T(8,128)S(1)}, u32[]{:S(2)}, u32[]{:S(2)}) collective-permute-start(f32[16,128]{1,0:T(8,128)S(1)} %convolution_add_fusion.4), channel_id=1, source_target_pairs={{1,0},{2,1},{3,2},{5,4},{6,5},{7,6},{9,8},{10,9},{11,10},{13,12},{... | collective-permute-start | bytes 24584 | tf_op jit(solution)/shard_map/while/body/eval_jaxpr/ppermute | solution.py:12
  24.4 5.1 %collective-permute-done = f32[16,128]{1,0:T(8,128)S(1)} collective-permute-done((f32[16,128]{1,0:T(8,128)S(1)}, f32[16,128]{1,0:T(8,128)S(1)}, u32[]{:S(2)}, u32[]{:S(2)}) %collective-permute-start) | collective-permute-done | bytes 8224 | tf_op jit(solution)/shard_map/while/body/eval_jaxpr/ppermute | solution.py:12
  30.0 1.4 %convolution_bitcast_fusion.5 = f32[16,128]{1,0:T(8,128)S(1)} fusion(f32[4,16,256]{2,1,0:T(8,128)S(1)} %fusion.14, f32[4,256,128]{2,1,0:T(8,128)} %param.23), kind=kOutput, calls=%fused_computation.19 | convolution fusion | flops 25165824 | bytes 598016 | tf_op jit(solution)/shard_map/tsc,tck->sk/dot_general | solution.py:71
  31.4 14.2 %all_gather.6 = f32[128,128]{1,0:T(8,128)S(1)} all-gather(f32[16,128]{1,0:T(8,128)S(1)} %convolution_bitcast_fusion.5), channel_id=1, replica_groups=mesh['sub'=8,'front'=4] {'sub'}, dimensions={0}, use_global_device_ids=true | all-gather | bytes 73728 | tf_op jit(solution)/shard_map/all_gather | solution.py:72
  45.6 10.6 %all-gather = f32[512,128]{1,0:T(8,128)S(1)} all-gather(f32[128,128]{1,0:T(8,128)S(1)} %all_gather.6), channel_id=2, replica_groups=mesh['sub'=8,'front'=4] {'front'}, dimensions={0}, use_global_device_ids=true | all-gather | bytes 327680 | tf_op jit(solution)/shard_map/all_gather | solution.py:73
  56.7 6.9 %fusion.6 = f32[8,128,256]{2,1,0:T(8,128)S(1)} fusion(f32[8,128,256]{2,1,0:T(8,128)} %param.24, f32[1,4,8,256,128]{4,3,2,1,0:T(8,128)} %param.29, f32[4,128,128]{2,1,0:T(8,128)S(1)} %gather_fusion, f32[4,128]{1,0:T(4,128)S(1)} %fusion.21), kind=kOutput, calls=%fused_computation.8 | convolution fusion | flops 1610940416 | bytes 6555648 | tf_op jit(solution)/shard_map/msk,mtbk->tsb/dot_general | solution.py:75
  63.6 1.4 %fusion.25 = f32[8,128,256]{2,1,0:T(8,128)S(1)} fusion(f32[8,128,256]{2,1,0:T(8,128)S(1)} %fusion.6, f32[8,256,256]{2,1,0:T(8,128)S(1)} %copy-done), kind=kOutput, calls=%fused_computation.36 | convolution fusion | flops 805306368 | bytes 4194304 | tf_op jit(solution)/shard_map/tsb,tbc->tsc/dot_general | solution.py:27
  66.3 2.0 %fusion.26 = f32[8,128,256]{2,1,0:T(8,128)S(1)} fusion(f32[8,256,128]{2,1,0:T(8,128)S(1)} %copy-done.5, f32[8,256,256]{2,1,0:T(8,128)S(1)} %copy-done), kind=kOutput, calls=%fused_computation.37 | convolution fusion | flops 805306368 | bytes 4194304 | tf_op jit(solution)/shard_map/tbk,tbc->tkc/dot_general | solution.py:21
  70.5 19.1 %while.21 = (s32[]{:T(128)}, f32[128,128]{1,0:T(8,128)S(1)}, f32[128,128]{1,0:T(8,128)S(1)}, f32[128,128]{1,0:T(8,128)S(1)}, s32[]{:T(128)}) while((s32[]{:T(128)}, f32[128,128]{1,0:T(8,128)S(1)}, f32[128,128]{1,0:T(8,128)S(1)}, f32[128,128]{1,0:T(8,128)S(1)}, s32[]{:T(128)}) %tuple.38), condition=%wide.region_3.0_spmd, body=%wide.region_2.0_spmd.sunk | while | flops 25182208 | bytes 524389 | solution.py:41
  70.7 1.3 %collective-permute-start.1 = (f32[128,128]{1,0:T(8,128)S(1)}, f32[128,128]{1,0:T(8,128)S(1)}, u32[]{:S(2)}, u32[]{:S(2)}) collective-permute-start(f32[128,128]{1,0:T(8,128)S(1)} %convolution_add_fusion.5), channel_id=1, source_target_pairs={{1,0},{2,1},{3,2},{5,4},{6,5},{7,6},{9,8},{10,9},{11,10},{13,12},{... | collective-permute-start | bytes 196616 | tf_op jit(solution)/shard_map/while/body/eval_jaxpr/ppermute | solution.py:12
  72.0 4.9 %collective-permute-done.1 = f32[128,128]{1,0:T(8,128)S(1)} collective-permute-done((f32[128,128]{1,0:T(8,128)S(1)}, f32[128,128]{1,0:T(8,128)S(1)}, u32[]{:S(2)}, u32[]{:S(2)}) %collective-permute-start.1) | collective-permute-done | bytes 65568 | tf_op jit(solution)/shard_map/while/body/eval_jaxpr/ppermute | solution.py:12
  77.0 1.3 %collective-permute-start.1 = (f32[128,128]{1,0:T(8,128)S(1)}, f32[128,128]{1,0:T(8,128)S(1)}, u32[]{:S(2)}, u32[]{:S(2)}) collective-permute-start(f32[128,128]{1,0:T(8,128)S(1)} %convolution_add_fusion.5), channel_id=1, source_target_pairs={{1,0},{2,1},{3,2},{5,4},{6,5},{7,6},{9,8},{10,9},{11,10},{13,12},{... | collective-permute-start | bytes 196616 | tf_op jit(solution)/shard_map/while/body/eval_jaxpr/ppermute | solution.py:12
  78.4 4.9 %collective-permute-done.1 = f32[128,128]{1,0:T(8,128)S(1)} collective-permute-done((f32[128,128]{1,0:T(8,128)S(1)}, f32[128,128]{1,0:T(8,128)S(1)}, u32[]{:S(2)}, u32[]{:S(2)}) %collective-permute-start.1) | collective-permute-done | bytes 65568 | tf_op jit(solution)/shard_map/while/body/eval_jaxpr/ppermute | solution.py:12
  83.4 1.3 %collective-permute-start.1 = (f32[128,128]{1,0:T(8,128)S(1)}, f32[128,128]{1,0:T(8,128)S(1)}, u32[]{:S(2)}, u32[]{:S(2)}) collective-permute-start(f32[128,128]{1,0:T(8,128)S(1)} %convolution_add_fusion.5), channel_id=1, source_target_pairs={{1,0},{2,1},{3,2},{5,4},{6,5},{7,6},{9,8},{10,9},{11,10},{13,12},{... | collective-permute-start | bytes 196616 | tf_op jit(solution)/shard_map/while/body/eval_jaxpr/ppermute | solution.py:12
  84.7 4.9 %collective-permute-done.1 = f32[128,128]{1,0:T(8,128)S(1)} collective-permute-done((f32[128,128]{1,0:T(8,128)S(1)}, f32[128,128]{1,0:T(8,128)S(1)}, u32[]{:S(2)}, u32[]{:S(2)}) %collective-permute-start.1) | collective-permute-done | bytes 65568 | tf_op jit(solution)/shard_map/while/body/eval_jaxpr/ppermute | solution.py:12
  89.6 3.3 %fusion.5 = f32[8,128,256]{2,1,0:T(8,128)} fusion(f32[8,128,256]{2,1,0:T(8,128)S(1)} %fusion.25, f32[8,128,256]{2,1,0:T(8,128)} %copy-done.1, f32[128,128]{1,0:T(8,128)S(1)} %get-tuple-element.47), kind=kOutput, calls=%fused_computation.7 | convolution fusion | flops 402915328 | bytes 3211264 | tf_op jit(solution)/shard_map/sk,tkc->tsc/dot_general | solution.py:80
  (32 shorter events, 7.4 us)
Async XLA Ops:
  0.6 63.0 %copy-start = (f32[8,256,256]{2,1,0:T(8,128)S(1)}, f32[8,256,256]{2,1,0:T(8,128)}, u32[]{:S(2)}) copy-start(f32[8,256,256]{2,1,0:T(8,128)} %param.25) | copy-start | bytes 6291460
  0.6 8.4 %copy-start.4 = (f32[4,256,128]{2,1,0:T(8,128)S(1)}, f32[4,256,128]{2,1,0:T(8,128)}, u32[]{:S(2)}) copy-start(f32[4,256,128]{2,1,0:T(8,128)} %param.20) | copy-start | bytes 1572868
  0.7 6.3 %copy-start.3 = (f32[4,256,256]{2,1,0:T(8,128)S(1)}, f32[4,256,256]{2,1,0:T(8,128)}, u32[]{:S(2)}) copy-start(f32[4,256,256]{2,1,0:T(8,128)} %param.19) | copy-start | bytes 3145732
  9.9 6.5 %collective-permute-start = (f32[16,128]{1,0:T(8,128)S(1)}, f32[16,128]{1,0:T(8,128)S(1)}, u32[]{:S(2)}, u32[]{:S(2)}) collective-permute-start(f32[16,128]{1,0:T(8,128)S(1)} %convolution_add_fusion.4), channel_id=1, source_target_pairs={{1,0},{2,1},{3,2},{5,4},{6,5},{7,6},{9,8},{10,9},{11,10},{13,12},{... | collective-permute-start | bytes 24584 | tf_op jit(solution)/shard_map/while/body/eval_jaxpr/ppermute | solution.py:12
  16.5 6.5 %collective-permute-start = (f32[16,128]{1,0:T(8,128)S(1)}, f32[16,128]{1,0:T(8,128)S(1)}, u32[]{:S(2)}, u32[]{:S(2)}) collective-permute-start(f32[16,128]{1,0:T(8,128)S(1)} %convolution_add_fusion.4), channel_id=1, source_target_pairs={{1,0},{2,1},{3,2},{5,4},{6,5},{7,6},{9,8},{10,9},{11,10},{13,12},{... | collective-permute-start | bytes 24584 | tf_op jit(solution)/shard_map/while/body/eval_jaxpr/ppermute | solution.py:12
  23.1 6.5 %collective-permute-start = (f32[16,128]{1,0:T(8,128)S(1)}, f32[16,128]{1,0:T(8,128)S(1)}, u32[]{:S(2)}, u32[]{:S(2)}) collective-permute-start(f32[16,128]{1,0:T(8,128)S(1)} %convolution_add_fusion.4), channel_id=1, source_target_pairs={{1,0},{2,1},{3,2},{5,4},{6,5},{7,6},{9,8},{10,9},{11,10},{13,12},{... | collective-permute-start | bytes 24584 | tf_op jit(solution)/shard_map/while/body/eval_jaxpr/ppermute | solution.py:12
  30.0 33.7 %copy-start.6 = (f32[4,16,256]{2,1,0:T(8,128)}, f32[4,16,256]{2,1,0:T(8,128)S(1)}, u32[]{:S(2)}) copy-start(f32[4,16,256]{2,1,0:T(8,128)S(1)} %fusion.14) | copy-start | bytes 196612
  63.6 1.4 %copy-start.2 = (f32[8,256,128]{2,1,0:T(8,128)S(1)}, f32[8,256,128]{2,1,0:T(8,128)}, u32[]{:S(2)}) copy-start(f32[8,256,128]{2,1,0:T(8,128)} %param.26) | copy-start | bytes 3145732
  65.0 1.2 %copy-start.5 = (f32[8,256,128]{2,1,0:T(8,128)S(1)}, f32[8,256,128]{2,1,0:T(8,128)}, u32[]{:S(2)}) copy-start(f32[8,256,128]{2,1,0:T(8,128)} %param.27) | copy-start | bytes 3145732
  68.3 1.0 %copy-start.1 = (f32[8,128,256]{2,1,0:T(8,128)}, f32[8,128,256]{2,1,0:T(8,128)S(1)}, u32[]{:S(2)}) copy-start(f32[8,128,256]{2,1,0:T(8,128)S(1)} %fusion.26) | copy-start | bytes 3145732
  70.7 6.2 %collective-permute-start.1 = (f32[128,128]{1,0:T(8,128)S(1)}, f32[128,128]{1,0:T(8,128)S(1)}, u32[]{:S(2)}, u32[]{:S(2)}) collective-permute-start(f32[128,128]{1,0:T(8,128)S(1)} %convolution_add_fusion.5), channel_id=1, source_target_pairs={{1,0},{2,1},{3,2},{5,4},{6,5},{7,6},{9,8},{10,9},{11,10},{13,12},{... | collective-permute-start | bytes 196616 | tf_op jit(solution)/shard_map/while/body/eval_jaxpr/ppermute | solution.py:12
  77.0 6.2 %collective-permute-start.1 = (f32[128,128]{1,0:T(8,128)S(1)}, f32[128,128]{1,0:T(8,128)S(1)}, u32[]{:S(2)}, u32[]{:S(2)}) collective-permute-start(f32[128,128]{1,0:T(8,128)S(1)} %convolution_add_fusion.5), channel_id=1, source_target_pairs={{1,0},{2,1},{3,2},{5,4},{6,5},{7,6},{9,8},{10,9},{11,10},{13,12},{... | collective-permute-start | bytes 196616 | tf_op jit(solution)/shard_map/while/body/eval_jaxpr/ppermute | solution.py:12
  83.4 6.2 %collective-permute-start.1 = (f32[128,128]{1,0:T(8,128)S(1)}, f32[128,128]{1,0:T(8,128)S(1)}, u32[]{:S(2)}, u32[]{:S(2)}) collective-permute-start(f32[128,128]{1,0:T(8,128)S(1)} %convolution_add_fusion.5), channel_id=1, source_target_pairs={{1,0},{2,1},{3,2},{5,4},{6,5},{7,6},{9,8},{10,9},{11,10},{13,12},{... | collective-permute-start | bytes 196616 | tf_op jit(solution)/shard_map/while/body/eval_jaxpr/ppermute | solution.py:12
where the time goes:
time: 93.3 us; the launch traced here: 92.8 us
  waiting for transfers between devices  30 us (32%)
  matrix products  24.8 us (27%)
  blocking collectives  24.8 us (27%)
  starting transfers between devices  7.78 us (8%)
  between operations  2.36 us (3%)
  local copies, waits for them, and re-layouts  1.64 us (2%)
  other arithmetic  1.4 us (2%)
    ppermute x6, waiting for transfers between devices, shifted(): lax.ppermute(value, axis, [(source, source + steps) for source in range(i...  30 us
    all_gather x1, blocking collectives, body(): samples = lax.all_gather(projected, 'sub', axis=0, tiled=True)  14.2 us
    all_gather x1, blocking collectives, body(): all_projected = lax.all_gather(samples[None], 'front', axis=0, tiled=True)  10.6 us
    ppermute x6, starting transfers between devices, shifted(): lax.ppermute(value, axis, [(source, source + steps) for source in range(i...  7.78 us
    dot_general x1, matrix products, body(): update = jnp.einsum('msk,mtbk->tsb', chosen, couple[0], precision=PRECISE)  6.87 us
    dot_general x2, matrix products, operator_terms(): carried = jnp.einsum('tbk,tbc->tkc', leftward, inverse, precision=PRECISE)  4.15 us
    dot_general x1, matrix products, body(): jnp.einsum('sk,tkc->tsc', child_message, child_carried, precision=PRECISE)  3.26 us
    dot_general x2, matrix products, source_terms(): solved = jnp.einsum('tsb,tbc->tsc', source, inverse, precision=PRECISE)  3.25 us
  transfers between devices with their start and end apart: 6, of which 6 were waited for; matrix products, arithmetic and copies ran while one was open for 0% of the time, Pallas kernels for 0%

commit v1 on v0

v1 whole, which is shorter than its diff:
```python
import functools

import jax
import jax.numpy as jnp
from jax import lax
from jax.experimental import pallas as pl
from jax.experimental.pallas import tpu as pltpu
from jax.sharding import PartitionSpec as P

F32 = jnp.float32
BF16 = jnp.bfloat16
NN = ((1,), (0,))
NT = ((1,), (1,))


def split(value):
    high = value.astype(BF16)
    return high, (value - high.astype(F32)).astype(BF16)


def dot3(left, right, contract):
    def one(x, y):
        return lax.dot_general(x, y, (contract, ((), ())), preferred_element_type=F32)

    return one(left[0], right[0]) + (one(left[0], right[1]) + one(left[1], right[0]))


def dot(left, right, contract):
    return dot3(split(left), split(right), contract)


def kernel(
    front_count,
    sub_count,
    rank_root,
    rank_child,
    pattern,
    couple_rank,
    noise_root_hbm,
    inverse_root_hbm,
    up_root_hbm,
    left_root_hbm,
    basis_root_hbm,
    noise_child_hbm,
    inverse_child_hbm,
    up_child_hbm,
    left_child_hbm,
    couple_hbm,
    solved_root_hbm,
    solved_child_hbm,
    noise_root,
    inverse_root,
    up_root,
    left_root,
    basis_root,
    noise_child,
    inverse_child,
    up_child,
    left_child,
    couple,
    solved_root,
    solved_child,
    root_mixing,
    root_message,
    root_outgoing,
    projected,
    child_opening,
    child_factor,
    carried,
    mixings,
    openings,
    message,
    load_sem,
    store_sem,
    chain_sem,
    sub_send,
    sub_recv,
    front_send,
    front_recv,
    mixing_send,
    mixing_recv,
    opening_send,
    opening_recv,
):
    sub = lax.axis_index("sub")
    front = lax.axis_index("front")
    root_tiles, share, _ = noise_root.shape
    child_tiles = noise_child.shape[0]
    width = up_root.shape[-1]
    couplings = couple.shape[0]
    last = front_count - 1

    loads = {}
    for index, (name, source, target) in enumerate((
        ("inverse_root", inverse_root_hbm, inverse_root),
        ("up_root", up_root_hbm, up_root),
        ("basis_root", basis_root_hbm, basis_root),
        ("noise_root", noise_root_hbm, noise_root),
        ("left_root", left_root_hbm, left_root),
        ("inverse_child", inverse_child_hbm, inverse_child),
        ("up_child", up_child_hbm, up_child),
        ("noise_child", noise_child_hbm, noise_child),
        ("left_child", left_child_hbm, left_child),
        ("couple", couple_hbm.at[0], couple),
    )):
        loads[name] = pltpu.make_async_copy(source, target, load_sem.at[index])
        loads[name].start()

    barrier = pltpu.get_barrier_semaphore()
    for step in range(1, sub_count):
        pl.semaphore_signal(
            barrier, inc=1, device_id={"sub": lax.rem(sub + step, sub_count)}, device_id_type=pl.DeviceIdType.MESH
        )
    for step in range(1, front_count):
        pl.semaphore_signal(
            barrier, inc=1, device_id={"front": lax.rem(front + step, front_count)}, device_id_type=pl.DeviceIdType.MESH
        )

    lanes = lax.broadcasted_iota(jnp.int32, (1, width), 1)
    rows = lax.broadcasted_iota(jnp.int32, (width, width), 0)
    root_keep = (lanes < rank_root[0]).astype(F32)
    child_keep = (lanes < rank_child[0]).astype(F32)

    def remote(source, target, send, recv, axis, peer):
        return pltpu.make_async_remote_copy(
            src_ref=source,
            dst_ref=target,
            send_sem=send,
            recv_sem=recv,
            device_id={axis: peer},
            device_id_type=pl.DeviceIdType.MESH,
        )

    for name in ("inverse_root", "up_root", "basis_root", "noise_root"):
        loads[name].wait()
    solved_bases = []
    opening = jnp.zeros((share, 2 * width), F32)
    for tile in range(root_tiles):
        bases = jnp.concatenate([up_root[tile], basis_root[tile]], axis=1)
        solved_basis = dot(inverse_root[tile], bases, NN)
        opening = opening + dot(noise_root[tile], solved_basis, NN)
        solved_bases.append(solved_basis)
    pl.semaphore_wait(barrier, sub_count + front_count - 2)

    chain = remote(
        root_outgoing, root_message, chain_sem.at[0], chain_sem.at[1], "front", lax.rem(front + last, front_count)
    )

    @pl.when(front == last)
    def _():
        root_message[...] = jnp.zeros_like(root_message)
        root_outgoing[...] = root_keep * opening[:, :width]
        chain.start()

    loads["left_root"].wait()
    mixing = jnp.zeros((2 * width, width), F32)
    for tile in range(root_tiles):
        mixing = mixing + dot(solved_bases[tile].T, left_root[tile], NN)
    root_mixing[...] = mixing

    @pl.when(front < last)
    def _():
        chain.wait_recv()

    arrived = root_message[...]
    both = opening - dot(arrived, root_mixing[...], NT)

    @pl.when(jnp.logical_and(front < last, front > 0))
    def _():
        root_outgoing[...] = root_keep * both[:, :width]
        chain.start()

    mine = pl.ds(pl.multiple_of(sub * share, share), share)
    projected[front, mine, :] = both[:, width:]
    for step in range(1, sub_count):
        block = projected.at[front, mine, :]
        remote(block, block, sub_send.at[step], sub_recv.at[sub], "sub", lax.rem(sub + step, sub_count)).start()

    for name in ("inverse_child", "up_child", "noise_child", "left_child", "couple"):
        loads[name].wait()
    child_opening[...] = jnp.zeros_like(child_opening)
    child_factor[...] = jnp.zeros_like(child_factor)

    def prepare(tile, _):
        solved_basis = dot(inverse_child[tile], up_child[tile], NN)
        child_opening[...] += dot(noise_child[tile], solved_basis, NN)
        columns = jnp.concatenate([left_child[tile]] + [couple[m, tile] for m in range(couplings)], axis=1)
        child_factor[...] += dot(solved_basis.T, columns, NN)
        return 0

    lax.fori_loop(0, child_tiles // 2, prepare, 0)

    for step in range(1, sub_count):
        peer = lax.rem(sub + step, sub_count)
        block = projected.at[front, pl.ds(pl.multiple_of(peer * share, share), share), :]
        remote(block, block, sub_send.at[step], sub_recv.at[peer], "sub", peer).wait_recv()
    for step in range(1, front_count):
        block = projected.at[front]
        remote(
            block, block, front_send.at[step], front_recv.at[front], "front", lax.rem(front + step, front_count)
        ).start()

    lax.fori_loop(child_tiles // 2, child_tiles, prepare, 0)

    mixings[front] = jnp.where(rows < rank_child[0], -child_factor[:, :width], 0.0)
    for peer in range(last):

        @pl.when(jnp.logical_and(peer < front, front < last))
        def _():
            block = mixings.at[front]
            remote(block, block, mixing_send.at[peer], mixing_recv.at[front], "front", peer).start()

    for tile in range(root_tiles):
        reduced = noise_root[tile] - dot(arrived, left_root[tile], NT)
        solved_root[tile] = dot(reduced, inverse_root[tile], NN)
    root_store = pltpu.make_async_copy(solved_root, solved_root_hbm, store_sem.at[0])
    root_store.start()

    for step in range(1, front_count):
        peer = lax.rem(front + step, front_count)
        block = projected.at[peer]
        remote(block, block, front_send.at[step], front_recv.at[peer], "front", peer).wait_recv()

    chosen = jnp.concatenate(
        [
            projected[pattern[0, m]] * (lanes < couple_rank[0, m]).astype(F32)
            for m in range(couplings)
        ],
        axis=1,
    )
    chosen = split(chosen)
    openings[front] = child_keep * (child_opening[...] - dot3(chosen, split(child_factor[:, width:]), NT))
    for peer in range(last):

        @pl.when(peer < front)
        def _():
            block = openings.at[front]
            remote(block, block, opening_send.at[peer], opening_recv.at[front], "front", peer).start()

    def solve(tile, _):
        inverse = split(inverse_child[tile])
        columns = jnp.concatenate([couple[m, tile] for m in range(couplings)], axis=1)
        source = noise_child[tile] - dot3(chosen, split(columns), NT)
        solved_child[tile] = dot3(split(source), inverse, NN)
        carried[tile] = dot3(split(left_child[tile].T), inverse, NN)
        return 0

    lax.fori_loop(0, child_tiles, solve, 0)

    message[...] = jnp.zeros_like(message)
    for panel in range(last, 0, -1):

        @pl.when(front < panel)
        def _():
            if panel < last:
                block = mixings.at[panel]
                remote(block, block, mixing_send.at[0], mixing_recv.at[panel], "front", panel).wait_recv()
            block = openings.at[panel]
            remote(block, block, opening_send.at[0], opening_recv.at[panel], "front", panel).wait_recv()
            if panel < last:
                message[...] = openings[panel] + dot(message[...], mixings[panel], NT)
            else:
                message[...] = openings[panel]

    incoming = split(message[...])
    stores = []
    for tile in range(child_tiles):
        solved_child[tile] -= dot3(incoming, split(carried[tile]), NN)
        stores.append(pltpu.make_async_copy(solved_child.at[tile], solved_child_hbm.at[tile], store_sem.at[1 + tile]))
        stores[-1].start()

    @pl.when(front > 0)
    def _():
        chain.wait_send()

    for step in range(1, sub_count):
        block = projected.at[front, mine, :]
        remote(block, block, sub_send.at[step], sub_recv.at[sub], "sub", lax.rem(sub + step, sub_count)).wait_send()
    for step in range(1, front_count):
        block = projected.at[front]
        remote(
            block, block, front_send.at[step], front_recv.at[front], "front", lax.rem(front + step, front_count)
        ).wait_send()
    for peer in range(last):

        @pl.when(jnp.logical_and(peer < front, front < last))
        def _():
            block = mixings.at[front]
            remote(block, block, mixing_send.at[peer], mixing_recv.at[front], "front", peer).wait_send()

        @pl.when(peer < front)
        def _():
            block = openings.at[front]
            remote(block, block, opening_send.at[peer], opening_recv.at[front], "front", peer).wait_send()

    root_store.wait()
    for store in stores:
        store.wait()


def body(
    front_count,
    sub_count,
    noise_root,
    inverse_root,
    up_root,
    left_root,
    rank_root,
    basis_root,
    noise_child,
    inverse_child,
    up_child,
    left_child,
    rank_child,
    couple,
    pattern,
    couple_rank,
):
    share = noise_root.shape[1]
    child_tiles, samples, _ = noise_child.shape
    order, width = up_root.shape[1:]
    couplings = couple.shape[1]
    arrays = (
        noise_root,
        inverse_root,
        up_root,
        left_root,
        basis_root,
        noise_child,
        inverse_child,
        up_child,
        left_child,
        couple,
    )
    dma = pltpu.SemaphoreType.DMA
    return pl.pallas_call(
        functools.partial(kernel, front_count, sub_count),
        out_shape=(
            jax.ShapeDtypeStruct(noise_root.shape, F32),
            jax.ShapeDtypeStruct(noise_child.shape, F32),
        ),
        in_specs=[pl.BlockSpec(memory_space=pltpu.SMEM)] * 4 + [pl.BlockSpec(memory_space=pl.ANY)] * len(arrays),
        out_specs=(pl.BlockSpec(memory_space=pl.ANY), pl.BlockSpec(memory_space=pl.ANY)),
        scratch_shapes=[pltpu.VMEM(array.shape, F32) for array in arrays[:-1]]
        + [
            pltpu.VMEM(couple.shape[1:], F32),
            pltpu.VMEM(noise_root.shape, F32),
            pltpu.VMEM(noise_child.shape, F32),
            pltpu.VMEM((2 * width, width), F32),
            pltpu.VMEM((share, width), F32),
            pltpu.VMEM((share, width), F32),
            pltpu.VMEM((front_count, samples, width), F32),
            pltpu.VMEM((samples, width), F32),
            pltpu.VMEM((width, (1 + couplings) * width), F32),
            pltpu.VMEM((child_tiles, width, order), F32),
            pltpu.VMEM((front_count, width, width), F32),
            pltpu.VMEM((front_count, samples, width), F32),
            pltpu.VMEM((samples, width), F32),
            dma((len(arrays),)),
            dma((1 + child_tiles,)),
            dma((2,)),
            dma((sub_count,)),
            dma((sub_count,)),
            dma((front_count,)),
            dma((front_count,)),
            dma((front_count,)),
            dma((front_count,)),
            dma((front_count,)),
            dma((front_count,)),
        ],
        compiler_params=pltpu.CompilerParams(
            collective_id=0, has_side_effects=True, vmem_limit_bytes=52 * 1024 * 1024
        ),
        name="matern_sample",
    )(rank_root, rank_child, pattern, couple_rank, *arrays)


def solution(mesh):
    placed = (
        P("front", "sub", None),
        P("front", None, None),
        P("front", None, None),
        P("front", None, None),
        P("front"),
        P("front", None, None),
        P(("sub", "front"), None, None),
        P(("sub", "front"), None, None),
        P(("sub", "front"), None, None),
        P(("sub", "front"), None, None),
        P(("sub", "front")),
        P(("sub", "front"), None, None, None, None),
        P(("sub", "front"), None),
        P(("sub", "front"), None),
    )
    return jax.shard_map(
        functools.partial(body, mesh.shape["front"], mesh.shape["sub"]),
        mesh=mesh,
        in_specs=placed,
        out_specs=(P("front", "sub", None), P(("sub", "front"), None, None)),
        check_vma=False,
    )
```

time: 93.3 us -> 42.6 us (0.46)
  Pallas kernels: 0 us -> 32.1 us
  waiting for transfers between devices: 30 us -> 0 us
  matrix products: 24.8 us -> 0 us
  blocking collectives: 24.8 us -> 0 us
  starting transfers between devices: 7.78 us -> 0 us
  local copies, waits for them, and re-layouts: 1.64 us -> 8.17 us
  other arithmetic: 1.4 us -> 0 us
    pallas_call x0 -> x1, Pallas kernels: none -> 32.1 us  [body(): pl.pallas_call(functools.partial(kernel, front_count, sub_count), out_sha...]
    ppermute x6 -> x0, waiting for transfers between devices: 30 us -> none  [shifted(): lax.ppermute(value, axis, [(source, source + steps) for source in range(i...]
    all_gather x2 -> x0, blocking collectives: 24.8 us -> none  [the longest x1 14.2 us: body(): samples = lax.all_gather(projected, 'sub', axis=0, tiled=True)]
    dot_general x18 -> x0, matrix products: 24.8 us -> none  [the longest x1 6.87 us: body(): update = jnp.einsum('msk,mtbk->tsb', chosen, couple[0], precision=PRECISE)]
    ppermute x6 -> x0, starting transfers between devices: 7.78 us -> none  [shifted(): lax.ppermute(value, axis, [(source, source + steps) for source in range(i...]
    unnamed x14, local copies, waits for them, and re-layouts: 1.06 us -> 8.17 us
  transfers between devices with their start and end apart: 6 -> 0, of which waited for: 6 -> 0; matrix products, arithmetic and copies ran while one was open for 0% -> 0% of each run, Pallas kernels for 0% -> 0%
where the time goes in v1:
time: 42.6 us; the launch traced here: 42.2 us
  Pallas kernels  32.1 us (75%)
  local copies, waits for them, and re-layouts  8.17 us (19%)
  between operations  1.95 us (5%)
    pallas_call x1, Pallas kernels, body(): pl.pallas_call(functools.partial(kernel, front_count, sub_count), out_sha...  32.1 us
    unnamed x14, local copies, waits for them, and re-layouts  8.17 us

profile of v1, /device:TPU:0, one launch (start us, length us, event | category | flops | bytes accessed | tf_op | source)
XLA Modules:
  0.0 42.2 jit_solution(10634021710091824841)
XLA Ops:
  1.9 0.0 copy-start
  1.9 1.0 %copy-done = f32[4,256,128]{2,1,0:T(8,128)S(1)} copy-done((f32[4,256,128]{2,1,0:T(8,128)S(1)}, f32[4,256,128]{2,1,0:T(8,128)}, u32[]{:S(2)}) %copy-start) | copy-done | bytes 524312
  3.0 0.0 copy-start.1
  3.0 1.0 %copy-done.1 = f32[4,256,128]{2,1,0:T(8,128)S(1)} copy-done((f32[4,256,128]{2,1,0:T(8,128)S(1)}, f32[4,256,128]{2,1,0:T(8,128)}, u32[]{:S(2)}) %copy-start.1) | copy-done | bytes 524312
  4.0 0.0 copy-start.2
  4.0 1.0 %copy-done.2 = f32[4,256,128]{2,1,0:T(8,128)S(1)} copy-done((f32[4,256,128]{2,1,0:T(8,128)S(1)}, f32[4,256,128]{2,1,0:T(8,128)}, u32[]{:S(2)}) %copy-start.2) | copy-done | bytes 524312
  5.1 0.0 copy-start.3
  5.1 0.8 %copy-done.3 = f32[4,16,256]{2,1,0:T(8,128)S(1)} copy-done((f32[4,16,256]{2,1,0:T(8,128)S(1)}, f32[4,16,256]{2,1,0:T(8,128)}, u32[]{:S(2)}) %copy-start.3) | copy-done | bytes 65560
  5.9 0.0 copy-start.4
  5.9 0.7 %copy-done.4 = s32[1,4]{1,0:T(1,128)S(1)} copy-done((s32[1,4]{1,0:T(1,128)S(1)}, s32[1,4]{1,0:T(1,128)}, u32[]{:S(2)}) %copy-start.4) | copy-done | bytes 40
  6.5 0.0 copy-start.5
  6.5 0.7 %copy-done.5 = s32[1,4]{1,0:T(1,128)S(1)} copy-done((s32[1,4]{1,0:T(1,128)S(1)}, s32[1,4]{1,0:T(1,128)}, u32[]{:S(2)}) %copy-start.5) | copy-done | bytes 40
  7.2 32.1 %matern_sample.1 = (f32[4,16,256]{2,1,0:T(8,128)S(1)}, f32[8,128,256]{2,1,0:T(8,128)}) custom-call(s32[1]{0:T(128)S(6)} %copy.18.rank_root, s32[1]{0:T(128)S(6)} %copy.19.rank_child, s32[1,4]{1,0:T(1,128)S(1)} %copy-done.4, s32[1,4]{1,0:T(1,128)S(1)} %copy-done.5, f32[4,16,256]{2,1,0:T(8,128)S(1)} %copy-done.3, f32[4,256,256]{2,1,0:T(8,128)} %inverse_root_hbm.1, ...), custom_call_target="tpu_custom_call" | custom-call | tf_op jit(solution)/shard_map/matern_sample/pallas_call | solution.py:336
  39.3 0.6 %copy.20 = f32[4,16,256]{2,1,0:T(8,128)} copy(f32[4,16,256]{2,1,0:T(8,128)S(1)} %get-tuple-element.4) | data formatting | bytes 131072
  40.0 2.3 %copy.21 = f32[8,128,256]{2,1,0:T(8,128)} copy(f32[8,128,256]{2,1,0:T(8,128)} %get-tuple-element.5) | data formatting | bytes 2097152
Async XLA Ops:
  1.9 1.0 %copy-start = (f32[4,256,128]{2,1,0:T(8,128)S(1)}, f32[4,256,128]{2,1,0:T(8,128)}, u32[]{:S(2)}) copy-start(f32[4,256,128]{2,1,0:T(8,128)} %up_root_hbm.1) | copy-start | bytes 1572868
  3.0 1.0 %copy-start.1 = (f32[4,256,128]{2,1,0:T(8,128)S(1)}, f32[4,256,128]{2,1,0:T(8,128)}, u32[]{:S(2)}) copy-start(f32[4,256,128]{2,1,0:T(8,128)} %left_root_hbm.1) | copy-start | bytes 1572868
  4.0 1.0 %copy-start.2 = (f32[4,256,128]{2,1,0:T(8,128)S(1)}, f32[4,256,128]{2,1,0:T(8,128)}, u32[]{:S(2)}) copy-start(f32[4,256,128]{2,1,0:T(8,128)} %basis_root_hbm.1) | copy-start | bytes 1572868
  5.1 0.8 %copy-start.3 = (f32[4,16,256]{2,1,0:T(8,128)S(1)}, f32[4,16,256]{2,1,0:T(8,128)}, u32[]{:S(2)}) copy-start(f32[4,16,256]{2,1,0:T(8,128)} %noise_root_hbm.1) | copy-start | bytes 196612
  5.9 0.7 %copy-start.4 = (s32[1,4]{1,0:T(1,128)S(1)}, s32[1,4]{1,0:T(1,128)}, u32[]{:S(2)}) copy-start(s32[1,4]{1,0:T(1,128)} %pattern.1) | copy-start | bytes 52
  6.5 0.7 %copy-start.5 = (s32[1,4]{1,0:T(1,128)S(1)}, s32[1,4]{1,0:T(1,128)}, u32[]{:S(2)}) copy-start(s32[1,4]{1,0:T(1,128)} %couple_rank.1) | copy-start | bytes 52

commit v2 on v1

--- a/solution.py
+++ b/solution.py
@@ -22,7 +22,15 @@
     def one(x, y):
         return lax.dot_general(x, y, (contract, ((), ())), preferred_element_type=F32)
 
-    return one(left[0], right[0]) + (one(left[0], right[1]) + one(left[1], right[0]))
+    rows = left[0].shape[0]
+    side = 1 - contract[1][0]
+    columns = right[0].shape[side]
+    stacked = jnp.concatenate(left, axis=0)
+    if columns <= 128:
+        both = one(stacked, jnp.concatenate(right, axis=side))
+        return both[:rows, :columns] + (both[rows:, :columns] + both[:rows, columns:])
+    both = one(stacked, right[0])
+    return both[:rows] + (both[rows:] + one(left[0], right[1]))
 
 
 def dot(left, right, contract):
@@ -32,10 +40,10 @@
 def kernel(
     front_count,
     sub_count,
-    rank_root,
-    rank_child,
-    pattern,
-    couple_rank,
+    rank_root_hbm,
+    rank_child_hbm,
+    pattern_hbm,
+    couple_rank_hbm,
     noise_root_hbm,
     inverse_root_hbm,
     up_root_hbm,
@@ -48,6 +56,10 @@
     couple_hbm,
     solved_root_hbm,
     solved_child_hbm,
+    rank_root,
+    rank_child,
+    pattern,
+    couple_rank,
     noise_root,
     inverse_root,
     up_root,
@@ -66,7 +78,8 @@
     projected,
     child_opening,
     child_factor,
-    carried,
+    carried_high,
+    carried_low,
     mixings,
     openings,
     message,
@@ -92,6 +105,10 @@
 
     loads = {}
     for index, (name, source, target) in enumerate((
+        ("rank_root", rank_root_hbm, rank_root),
+        ("rank_child", rank_child_hbm, rank_child),
+        ("pattern", pattern_hbm, pattern),
+        ("couple_rank", couple_rank_hbm, couple_rank),
         ("inverse_root", inverse_root_hbm, inverse_root),
         ("up_root", up_root_hbm, up_root),
         ("basis_root", basis_root_hbm, basis_root),
@@ -118,6 +135,8 @@
 
     lanes = lax.broadcasted_iota(jnp.int32, (1, width), 1)
     rows = lax.broadcasted_iota(jnp.int32, (width, width), 0)
+    for name in ("rank_root", "rank_child", "pattern", "couple_rank"):
+        loads[name].wait()
     root_keep = (lanes < rank_root[0]).astype(F32)
     child_keep = (lanes < rank_child[0]).astype(F32)
 
@@ -241,8 +260,9 @@
         inverse = split(inverse_child[tile])
         columns = jnp.concatenate([couple[m, tile] for m in range(couplings)], axis=1)
         source = noise_child[tile] - dot3(chosen, split(columns), NT)
-        solved_child[tile] = dot3(split(source), inverse, NN)
-        carried[tile] = dot3(split(left_child[tile].T), inverse, NN)
+        together = dot3(split(jnp.concatenate([source, left_child[tile].T], axis=0)), inverse, NN)
+        solved_child[tile] = together[: source.shape[0]]
+        carried_high[tile], carried_low[tile] = split(together[source.shape[0] :])
         return 0
 
     lax.fori_loop(0, child_tiles, solve, 0)
@@ -265,7 +285,7 @@
     incoming = split(message[...])
     stores = []
     for tile in range(child_tiles):
-        solved_child[tile] -= dot3(incoming, split(carried[tile]), NN)
+        solved_child[tile] -= dot3(incoming, (carried_high[tile], carried_low[tile]), NN)
         stores.append(pltpu.make_async_copy(solved_child.at[tile], solved_child_hbm.at[tile], store_sem.at[1 + tile]))
         stores[-1].start()
 
@@ -336,12 +356,13 @@
     return pl.pallas_call(
         functools.partial(kernel, front_count, sub_count),
         out_shape=(
-            jax.ShapeDtypeStruct(noise_root.shape, F32),
-            jax.ShapeDtypeStruct(noise_child.shape, F32),
+            pltpu.VMEM(noise_root.shape, F32),
+            pltpu.VMEM(noise_child.shape, F32),
         ),
-        in_specs=[pl.BlockSpec(memory_space=pltpu.SMEM)] * 4 + [pl.BlockSpec(memory_space=pl.ANY)] * len(arrays),
+        in_specs=[pl.BlockSpec(memory_space=pltpu.HBM)] * (4 + len(arrays)),
         out_specs=(pl.BlockSpec(memory_space=pl.ANY), pl.BlockSpec(memory_space=pl.ANY)),
-        scratch_shapes=[pltpu.VMEM(array.shape, F32) for array in arrays[:-1]]
+        scratch_shapes=[pltpu.SMEM(array.shape, jnp.int32) for array in (rank_root, rank_child, pattern, couple_rank)]
+        + [pltpu.VMEM(array.shape, F32) for array in arrays[:-1]]
         + [
             pltpu.VMEM(couple.shape[1:], F32),
             pltpu.VMEM(noise_root.shape, F32),
@@ -352,11 +373,12 @@
             pltpu.VMEM((front_count, samples, width), F32),
             pltpu.VMEM((samples, width), F32),
             pltpu.VMEM((width, (1 + couplings) * width), F32),
-            pltpu.VMEM((child_tiles, width, order), F32),
+            pltpu.VMEM((child_tiles, width, order), BF16),
+            pltpu.VMEM((child_tiles, width, order), BF16),
             pltpu.VMEM((front_count, width, width), F32),
             pltpu.VMEM((front_count, samples, width), F32),
             pltpu.VMEM((samples, width), F32),
-            dma((len(arrays),)),
+            dma((4 + len(arrays),)),
             dma((1 + child_tiles,)),
             dma((2,)),
             dma((sub_count,)),
@@ -369,7 +391,7 @@
             dma((front_count,)),
         ],
         compiler_params=pltpu.CompilerParams(
-            collective_id=0, has_side_effects=True, vmem_limit_bytes=52 * 1024 * 1024
+            collective_id=0, has_side_effects=True, vmem_limit_bytes=64 * 1024 * 1024 - 4 * (noise_root.size + noise_child.size) - (1 << 20)
         ),
         name="matern_sample",
     )(rank_root, rank_child, pattern, couple_rank, *arrays)

time: 42.6 us -> 36.8 us (0.86)
  local copies, waits for them, and re-layouts: 8.17 us -> 1.6 us
  Pallas kernels: 32.1 us -> 33.1 us
    unnamed x14 -> x2, local copies, waits for them, and re-layouts: 8.17 us -> 1.6 us
    pallas_call x1, Pallas kernels: 32.1 us -> 33.1 us  [body(): pl.pallas_call(functools.partial(kernel, front_count, sub_count), out_sha...]
where the time goes in v2:
time: 36.8 us; the launch traced here: 36.6 us
  Pallas kernels  33.1 us (90%)
  between operations  1.93 us (5%)
  local copies, waits for them, and re-layouts  1.6 us (4%)
    pallas_call x1, Pallas kernels, body(): pl.pallas_call(functools.partial(kernel, front_count, sub_count), out_sha...  33.1 us
    unnamed x2, local copies, waits for them, and re-layouts  1.6 us

profile of v2, /device:TPU:0, one launch (start us, length us, event | category | flops | bytes accessed | tf_op | source)
XLA Modules:
  0.0 36.6 jit_solution(11467911213160065362)
XLA Ops:
  1.9 33.1 %matern_sample.1 = (f32[4,16,256]{2,1,0:T(8,128)S(1)}, f32[8,128,256]{2,1,0:T(8,128)S(1)}) custom-call(s32[1]{0:T(128)S(6)} %copy.20.rank_root_hbm, s32[1]{0:T(128)S(6)} %copy.21.rank_child_hbm, s32[1,4]{1,0:T(1,128)} %pattern_hbm.1, s32[1,4]{1,0:T(1,128)} %couple_rank_hbm.1, f32[4,16,256]{2,1,0:T(8,128)} %noise_root_hbm.1, f32[4,256,256]{2,1,0:T(8,128)} %inverse_root_hbm.1, ...), custom_call_target="tpu_custom_call" | custom-call | tf_op jit(solution)/shard_map/matern_sample/pallas_call | solution.py:356
  35.0 0.6 %copy.18 = f32[4,16,256]{2,1,0:T(8,128)} copy(f32[4,16,256]{2,1,0:T(8,128)S(1)} %get-tuple-element.2) | data formatting | bytes 131072
  35.7 1.0 %copy.19 = f32[8,128,256]{2,1,0:T(8,128)} copy(f32[8,128,256]{2,1,0:T(8,128)S(1)} %get-tuple-element.3) | data formatting | bytes 2097152

commit v3 on v2

--- a/solution.py
+++ b/solution.py
@@ -72,7 +72,6 @@
     couple,
     solved_root,
     solved_child,
-    root_mixing,
     root_message,
     root_outgoing,
     projected,
@@ -175,14 +174,14 @@
     mixing = jnp.zeros((2 * width, width), F32)
     for tile in range(root_tiles):
         mixing = mixing + dot(solved_bases[tile].T, left_root[tile], NN)
-    root_mixing[...] = mixing
+    mixing = split(mixing.T)
 
     @pl.when(front < last)
     def _():
         chain.wait_recv()
 
     arrived = root_message[...]
-    both = opening - dot(arrived, root_mixing[...], NT)
+    both = opening - dot3(split(arrived), mixing, NN)
 
     @pl.when(jnp.logical_and(front < last, front > 0))
     def _():
@@ -207,19 +206,20 @@
         child_factor[...] += dot(solved_basis.T, columns, NN)
         return 0
 
-    lax.fori_loop(0, child_tiles // 2, prepare, 0)
-
-    for step in range(1, sub_count):
-        peer = lax.rem(sub + step, sub_count)
-        block = projected.at[front, pl.ds(pl.multiple_of(peer * share, share), share), :]
-        remote(block, block, sub_send.at[step], sub_recv.at[peer], "sub", peer).wait_recv()
-    for step in range(1, front_count):
-        block = projected.at[front]
-        remote(
-            block, block, front_send.at[step], front_recv.at[front], "front", lax.rem(front + step, front_count)
-        ).start()
-
-    lax.fori_loop(child_tiles // 2, child_tiles, prepare, 0)
+    def handed(step, pair, peer, panel):
+        block = projected.at[panel, pl.ds(pl.multiple_of(pair * 2 * share, 2 * share), 2 * share), :]
+        return remote(block, block, front_send.at[pair, step], front_recv.at[pair, panel], "front", peer)
+
+    pairs = sub_count // 2
+    for turn in range(pairs):
+        pair = lax.rem(sub // 2 + turn, pairs)
+        peers = [2 * pair, 2 * pair + 1] if turn > 0 else [sub + 1 - 2 * lax.rem(sub, 2)]
+        for peer in peers:
+            block = projected.at[front, pl.ds(pl.multiple_of(peer * share, share), share), :]
+            remote(block, block, sub_send.at[0], sub_recv.at[peer], "sub", peer).wait_recv()
+        for step in range(1, front_count):
+            handed(step, pair, lax.rem(front + step, front_count), front).start()
+        lax.fori_loop(child_tiles * turn // pairs, child_tiles * (turn + 1) // pairs, prepare, 0)
 
     mixings[front] = jnp.where(rows < rank_child[0], -child_factor[:, :width], 0.0)
     for peer in range(last):
@@ -235,10 +235,11 @@
     root_store = pltpu.make_async_copy(solved_root, solved_root_hbm, store_sem.at[0])
     root_store.start()
 
+    factor = split(child_factor[:, width:])
     for step in range(1, front_count):
         peer = lax.rem(front + step, front_count)
-        block = projected.at[peer]
-        remote(block, block, front_send.at[step], front_recv.at[peer], "front", peer).wait_recv()
+        for pair in range(pairs):
+            handed(step, pair, peer, peer).wait_recv()
 
     chosen = jnp.concatenate(
         [
@@ -248,7 +249,7 @@
         axis=1,
     )
     chosen = split(chosen)
-    openings[front] = child_keep * (child_opening[...] - dot3(chosen, split(child_factor[:, width:]), NT))
+    openings[front] = child_keep * (child_opening[...] - dot3(chosen, factor, NT))
     for peer in range(last):
 
         @pl.when(peer < front)
@@ -297,10 +298,8 @@
         block = projected.at[front, mine, :]
         remote(block, block, sub_send.at[step], sub_recv.at[sub], "sub", lax.rem(sub + step, sub_count)).wait_send()
     for step in range(1, front_count):
-        block = projected.at[front]
-        remote(
-            block, block, front_send.at[step], front_recv.at[front], "front", lax.rem(front + step, front_count)
-        ).wait_send()
+        for pair in range(pairs):
+            handed(step, pair, lax.rem(front + step, front_count), front).wait_send()
     for peer in range(last):
 
         @pl.when(jnp.logical_and(peer < front, front < last))
@@ -367,7 +366,6 @@
             pltpu.VMEM(couple.shape[1:], F32),
             pltpu.VMEM(noise_root.shape, F32),
             pltpu.VMEM(noise_child.shape, F32),
-            pltpu.VMEM((2 * width, width), F32),
             pltpu.VMEM((share, width), F32),
             pltpu.VMEM((share, width), F32),
             pltpu.VMEM((front_count, samples, width), F32),
@@ -383,8 +381,8 @@
             dma((2,)),
             dma((sub_count,)),
             dma((sub_count,)),
-            dma((front_count,)),
-            dma((front_count,)),
+            dma((sub_count // 2, front_count)),
+            dma((sub_count // 2, front_count)),
             dma((front_count,)),
             dma((front_count,)),
             dma((front_count,)),

time: 36.8 us -> 36.2 us (0.984)
  Pallas kernels: 33.1 us -> 32.5 us
    pallas_call x1, Pallas kernels: 33.1 us -> 32.5 us  [body(): pl.pallas_call(functools.partial(kernel, front_count, sub_count), out_sha...]
where the time goes in v3:
time: 36.2 us; the launch traced here: 36.1 us
  Pallas kernels  32.5 us (90%)
  between operations  1.93 us (5%)
  local copies, waits for them, and re-layouts  1.6 us (4%)
    pallas_call x1, Pallas kernels, body(): pl.pallas_call(functools.partial(kernel, front_count, sub_count), out_sha...  32.5 us
    unnamed x2, local copies, waits for them, and re-layouts  1.6 us

profile of v3, /device:TPU:0, one launch (start us, length us, event | category | flops | bytes accessed | tf_op | source)
XLA Modules:
  0.0 36.1 jit_solution(11410018247552654785)
XLA Ops:
  1.9 32.5 %matern_sample.1 = (f32[4,16,256]{2,1,0:T(8,128)S(1)}, f32[8,128,256]{2,1,0:T(8,128)S(1)}) custom-call(s32[1]{0:T(128)S(6)} %copy.20.rank_root_hbm, s32[1]{0:T(128)S(6)} %copy.21.rank_child_hbm, s32[1,4]{1,0:T(1,128)} %pattern_hbm.1, s32[1,4]{1,0:T(1,128)} %couple_rank_hbm.1, f32[4,16,256]{2,1,0:T(8,128)} %noise_root_hbm.1, f32[4,256,256]{2,1,0:T(8,128)} %inverse_root_hbm.1, ...), custom_call_target="tpu_custom_call" | custom-call | tf_op jit(solution)/shard_map/matern_sample/pallas_call | solution.py:355
  34.5 0.6 %copy.18 = f32[4,16,256]{2,1,0:T(8,128)} copy(f32[4,16,256]{2,1,0:T(8,128)S(1)} %get-tuple-element.2) | data formatting | bytes 131072
  35.1 1.0 %copy.19 = f32[8,128,256]{2,1,0:T(8,128)} copy(f32[8,128,256]{2,1,0:T(8,128)S(1)} %get-tuple-element.3) | data formatting | bytes 2097152
